TPU v7x, 128 devices: a whole 4x4x4 slice. The times are simulated.
128 devices in a mesh: dp: 128 (over z, y, x, core).
Axes of the slice: x: 4, y: 4, z: 4, core: 2. Of those that a mesh axis runs over, the one named last changes fastest.
Arguments:
- tokens: bfloat16 [16384, 768], P('dp'), may hold values from -6 to 6
- cotangent: bfloat16 [16384, 768], P('dp'), may hold values from -6 to 6
- lengths: int32 [128, 4], P('dp'), may hold values from 1 to 80, 128 in all within a row
- gains: float32 [2, 768], P(None, 'dp'), may hold values from 0.5 to 1.5
- gain_moment: float32 [2, 768], P(None, 'dp'), may hold values from -384 to 384
- qkv_weight: float32 [3, 768, 768], P(None, 'dp'), may hold values from -0.21875 to 0.21875
- out_weight: float32 [768, 768], P('dp'), may hold values from -0.625 to 0.625
- inner_weight: float32 [2, 768, 3072], P(None, 'dp'), may hold values from -0.21875 to 0.21875
- down_weight: float32 [3072, 768], P('dp'), may hold values from -0.109375 to 0.109375
- qkv_moment: float32 [3, 768, 768], P(None, 'dp'), may hold values from -224 to 224
- out_moment: float32 [768, 768], P('dp'), may hold values from -224 to 224
- inner_moment: float32 [2, 768, 3072], P(None, 'dp'), may hold values from -224 to 224
- down_moment: float32 [3072, 768], P('dp'), may hold values from -224 to 224
Outputs:
- block_output: bfloat16 [16384, 768], P('dp')
- input_grad: float32 [16384, 768], P('dp')
- gain_grad: float32 [2, 768], P(None, 'dp')
- gain_moment_new: float32 [2, 768], P(None, 'dp')
- gains_new: float32 [2, 768], P(None, 'dp')
- qkv_grad: float32 [3, 768, 768], P(None, 'dp')
- out_grad: float32 [768, 768], P('dp')
- inner_grad: float32 [2, 768, 3072], P(None, 'dp')
- down_grad: float32 [3072, 768], P('dp')
- qkv_new: float32 [3, 768, 768], P(None, 'dp')
- out_new: float32 [768, 768], P('dp')
- inner_new: float32 [2, 768, 3072], P(None, 'dp')
- down_new: float32 [3072, 768], P('dp')
- qkv_moment_new: float32 [3, 768, 768], P(None, 'dp')
- out_moment_new: float32 [768, 768], P('dp')
- inner_moment_new: float32 [2, 768, 3072], P(None, 'dp')
- down_moment_new: float32 [3072, 768], P('dp')
Inputs may be any that keep to these rules, and one draw needn't show every extreme that they name: Each row holds the lengths of the 4 sequences that fill one pack of 128 tokens in order; in every row the longest is exactly 80.
All inputs are finite; a program needn't handle non-finite values.
Results may differ from a plain program's by a relative error of at most 0.012.
The roundings to bfloat16 on the way count: a program that leaves them out, or rounds other values in their place, can miss the bound.
Values may be sent and summed in bfloat16 or wider, within the bound.
No kernel may reach another device: no remote copies, remote signals or barrier semaphores. Data moves between devices by JAX's collectives and lax.ppermute only.
A program may use at most 192 MiB of HBM per device.

v0:
```python
import math

import jax
import jax.numpy as jnp
from jax import lax
from jax.sharding import PartitionSpec as P

HEAD = 64
NS_ITERS = 2


EPSILON = 1e-06
ROPE_BASE = 10000.0
MOMENTUM = 0.95
GAIN_MOMENTUM = 0.9
MUON_RATE = 0.3
GAIN_RATE = 0.001
WEIGHT_DECAY = 0.1
POLY_LINEAR = 3.4445
POLY_CUBIC = -4.775
POLY_QUINTIC = 2.0315


def segment_table(lengths, count):
    ends = jnp.cumsum(lengths, dtype=jnp.int32)
    places = jnp.arange(count, dtype=jnp.int32)
    segment = jnp.sum((places[:, None] >= ends[None, :]).astype(jnp.int32), axis=1, dtype=jnp.int32)
    starts = ends - lengths
    slots = jnp.arange(lengths.shape[0], dtype=jnp.int32)
    first = jnp.sum(
        jnp.where(segment[:, None] == slots[None, :], starts[None, :], 0), axis=1, dtype=jnp.int32
    )
    return (segment, places - first)


def rotate(values, position, sign):
    half = values.shape[-1] // 2
    freq = ROPE_BASE ** (-jnp.arange(half, dtype=jnp.float32) / half)
    angle = position.astype(jnp.float32)[:, None] * freq[None, :]
    cosine = jnp.cos(angle)[:, None, :]
    sine = sign * jnp.sin(angle)[:, None, :]
    first = values[..., :half]
    second = values[..., half:]
    return jnp.concatenate(
        [first * cosine - second * sine, second * cosine + first * sine], axis=-1
    )


def norm_scale(values):
    return lax.rsqrt(jnp.mean(values * values, axis=-1, keepdims=True) + EPSILON)


def norm_backward(values, scale, gain, grad):
    scaled = grad * gain
    gain_part = jnp.sum(grad * values * scale, axis=0)
    value_part = scale * scaled - values * (scale * scale * scale) * jnp.mean(
        scaled * values, axis=-1, keepdims=True
    )
    return (value_part, gain_part)


def contract_rows(left, right):
    return lax.dot_general(
        left, right, (((0,), (0,)), ((), ())), preferred_element_type=jnp.float32
    )


def times_transpose(left, right):
    return lax.dot_general(
        left, right, (((1,), (1,)), ((), ())), preferred_element_type=jnp.float32
    )


def score_block(part_query, keys, part_segment, segment, part_places, places):
    factor = part_query.shape[-1] ** (-0.5)
    dots = jnp.einsum("qhd,khd->hqk", part_query, keys, preferred_element_type=jnp.float32) * factor
    allowed = (part_segment[:, None] == segment[None, :]) & (
        places[None, :] <= part_places[:, None]
    )
    return jnp.where(allowed[None], dots, -1e30)


def orthogonalize(moment):
    flip = moment.shape[0] > moment.shape[1]
    matrix = moment
    matrix = matrix / (jnp.sqrt(jnp.sum(matrix * matrix)) + 1e-07)
    for turn in range(NS_ITERS):
        square = jnp.dot(matrix, matrix.T, precision=lax.Precision.HIGHEST)
        poly = POLY_CUBIC * square + POLY_QUINTIC * jnp.dot(
            square, square, precision=lax.Precision.HIGHEST
        )
        matrix = POLY_LINEAR * matrix + jnp.dot(poly, matrix, precision=lax.Precision.HIGHEST)
    return matrix


def to_common(matrix, width, hidden_width):
    if matrix.shape[0] > matrix.shape[1]:
        matrix = matrix.T
    return jnp.pad(matrix, ((0, width - matrix.shape[0]), (0, hidden_width - matrix.shape[1])))


def from_common(result, shape):
    rows, cols = shape
    if rows > cols:
        return result.T
    return result[:, :cols]


def apply_step(weight, update, rows, cols):
    return (
        weight * (1.0 - MUON_RATE * WEIGHT_DECAY)
        - MUON_RATE * (0.2 * math.sqrt(max(rows, cols))) * update
    )


def per_device(
    tokens,
    cotangent,
    lengths,
    gains,
    gain_moment,
    qkv_weight,
    out_weight,
    inner_weight,
    down_weight,
    qkv_moment,
    out_moment,
    inner_moment,
    down_moment,
):
    devices = lax.axis_size("dp")
    device_index = lax.axis_index("dp")
    count = tokens.shape[0]
    width = tokens.shape[1]
    hidden_width = inner_weight.shape[2]
    heads = width // HEAD
    segment, position = segment_table(lengths[0], count)
    places = jnp.arange(count, dtype=jnp.int32)
    qkv_full, out_full, inner_full, down_full, gains_full = (
        lax.all_gather(qkv_weight.astype(jnp.bfloat16), "dp", axis=1, tiled=True),
        lax.all_gather(out_weight.astype(jnp.bfloat16), "dp", axis=0, tiled=True),
        lax.all_gather(inner_weight.astype(jnp.bfloat16), "dp", axis=1, tiled=True),
        lax.all_gather(down_weight.astype(jnp.bfloat16), "dp", axis=0, tiled=True),
        lax.all_gather(gains.astype(jnp.bfloat16), "dp", axis=1, tiled=True),
    )
    inputs = tokens.astype(jnp.float32)
    scale_one = norm_scale(inputs)
    normed = (inputs * scale_one * gains_full[0].astype(jnp.float32)).astype(jnp.bfloat16)
    query_raw = jnp.dot(normed, qkv_full[0], preferred_element_type=jnp.float32).reshape(
        count, heads, HEAD
    )
    keys_raw = jnp.dot(normed, qkv_full[1], preferred_element_type=jnp.float32).reshape(
        count, heads, HEAD
    )
    values = (
        jnp.dot(normed, qkv_full[2], preferred_element_type=jnp.float32)
        .astype(jnp.bfloat16)
        .reshape(count, heads, HEAD)
    )
    query = rotate(query_raw, position, 1.0).astype(jnp.bfloat16)
    keys = rotate(keys_raw, position, 1.0).astype(jnp.bfloat16)
    block = min(count, 512)
    blocks = count // block
    query_blocks = query.reshape(blocks, block, heads, HEAD)
    segment_blocks = segment.reshape(blocks, block)
    place_blocks = places.reshape(blocks, block)

    def forward_block(pieces):
        part_query, part_segment, part_places = pieces
        dots = score_block(part_query, keys, part_segment, segment, part_places, places)
        top = jnp.max(dots, axis=-1, keepdims=True)
        weights = jnp.exp(dots - top)
        total = jnp.sum(weights, axis=-1, keepdims=True)
        probs = (weights / total).astype(jnp.bfloat16)
        mixed_part = jnp.einsum("hqk,khd->qhd", probs, values, preferred_element_type=jnp.float32)
        return (mixed_part, (top + jnp.log(total))[..., 0])

    mixed_blocks, log_blocks = lax.map(forward_block, (query_blocks, segment_blocks, place_blocks))
    mixed = mixed_blocks.reshape(count, width).astype(jnp.bfloat16)
    branch = jnp.dot(mixed, out_full, preferred_element_type=jnp.float32)
    middle = inputs + branch
    scale_two = norm_scale(middle)
    normed_two = (middle * scale_two * gains_full[1].astype(jnp.float32)).astype(jnp.bfloat16)
    gate = jnp.dot(normed_two, inner_full[0], preferred_element_type=jnp.float32)
    upward = jnp.dot(normed_two, inner_full[1], preferred_element_type=jnp.float32)
    sigma = jax.nn.sigmoid(gate)
    activated = gate * sigma
    hidden = (activated * upward).astype(jnp.bfloat16)
    block_output = (middle + jnp.dot(hidden, down_full, preferred_element_type=jnp.float32)).astype(
        jnp.bfloat16
    )
    qkv_back, out_back, inner_back, down_back, gains_back = (
        lax.all_gather(qkv_weight.astype(jnp.bfloat16), "dp", axis=1, tiled=True),
        lax.all_gather(out_weight.astype(jnp.bfloat16), "dp", axis=0, tiled=True),
        lax.all_gather(inner_weight.astype(jnp.bfloat16), "dp", axis=1, tiled=True),
        lax.all_gather(down_weight.astype(jnp.bfloat16), "dp", axis=0, tiled=True),
        lax.all_gather(gains.astype(jnp.bfloat16), "dp", axis=1, tiled=True),
    )
    down_grad = contract_rows(hidden, cotangent)
    hidden_grad = times_transpose(cotangent, down_back)
    gate_grad = (hidden_grad * upward * (sigma * (1.0 + gate * (1.0 - sigma)))).astype(jnp.bfloat16)
    upward_grad = (hidden_grad * activated).astype(jnp.bfloat16)
    inner_grad = jnp.stack(
        [contract_rows(normed_two, gate_grad), contract_rows(normed_two, upward_grad)]
    )
    normed_two_grad = times_transpose(gate_grad, inner_back[0]) + times_transpose(
        upward_grad, inner_back[1]
    )
    middle_part, gain_two_grad = norm_backward(
        middle, scale_two, gains_back[1].astype(jnp.float32), normed_two_grad
    )
    middle_grad = cotangent.astype(jnp.float32) + middle_part
    branch_grad = middle_grad.astype(jnp.bfloat16)
    out_grad = contract_rows(mixed, branch_grad)
    mixed_grad = times_transpose(branch_grad, out_back).astype(jnp.bfloat16)
    grad_blocks = mixed_grad.reshape(blocks, block, heads, HEAD)

    def backward_block(carry, pieces):
        keys_sum, values_sum = carry
        part_query, part_grad, part_segment, part_places, part_log = pieces
        dots = score_block(part_query, keys, part_segment, segment, part_places, places)
        probs = jnp.exp(dots - part_log[..., None])
        values_sum = values_sum + jnp.einsum(
            "hqk,qhd->khd",
            probs.astype(jnp.bfloat16),
            part_grad,
            preferred_element_type=jnp.float32,
        )
        probs_grad = jnp.einsum(
            "qhd,khd->hqk", part_grad, values, preferred_element_type=jnp.float32
        )
        centre = jnp.sum(probs * probs_grad, axis=-1, keepdims=True)
        dots_grad = (probs * (probs_grad - centre) * part_query.shape[-1] ** (-0.5)).astype(
            jnp.bfloat16
        )
        query_part = jnp.einsum("hqk,khd->qhd", dots_grad, keys, preferred_element_type=jnp.float32)
        keys_sum = keys_sum + jnp.einsum(
            "hqk,qhd->khd", dots_grad, part_query, preferred_element_type=jnp.float32
        )
        return ((keys_sum, values_sum), query_part)

    zeros = jnp.zeros((count, heads, HEAD), jnp.float32)
    (keys_total, values_total), query_parts = lax.scan(
        backward_block,
        (zeros, zeros),
        (query_blocks, grad_blocks, segment_blocks, place_blocks, log_blocks),
    )
    query_grad = (
        rotate(query_parts.reshape(count, heads, HEAD), position, -1.0)
        .reshape(count, width)
        .astype(jnp.bfloat16)
    )
    keys_grad = rotate(keys_total, position, -1.0).reshape(count, width).astype(jnp.bfloat16)
    values_grad = values_total.reshape(count, width).astype(jnp.bfloat16)
    qkv_grad = jnp.stack(
        [
            contract_rows(normed, query_grad),
            contract_rows(normed, keys_grad),
            contract_rows(normed, values_grad),
        ]
    )
    normed_grad = (
        times_transpose(query_grad, qkv_back[0])
        + times_transpose(keys_grad, qkv_back[1])
        + times_transpose(values_grad, qkv_back[2])
    )
    input_part, gain_one_grad = norm_backward(
        inputs, scale_one, gains_back[0].astype(jnp.float32), normed_grad
    )
    input_grad = middle_grad + input_part
    gain_local = jnp.stack([gain_one_grad, gain_two_grad])
    qkv_sum, out_sum, inner_sum, down_sum, gain_sum = (
        lax.psum_scatter(qkv_grad, "dp", scatter_dimension=1, tiled=True),
        lax.psum_scatter(out_grad, "dp", scatter_dimension=0, tiled=True),
        lax.psum_scatter(inner_grad, "dp", scatter_dimension=1, tiled=True),
        lax.psum_scatter(down_grad, "dp", scatter_dimension=0, tiled=True),
        lax.psum_scatter(gain_local, "dp", scatter_dimension=1, tiled=True),
    )
    qkv_next = MOMENTUM * qkv_moment + qkv_sum
    out_next = MOMENTUM * out_moment + out_sum
    inner_next = MOMENTUM * inner_moment + inner_sum
    down_next = MOMENTUM * down_moment + down_sum
    spacing = devices // 8
    shapes = [
        (width, width),
        (width, width),
        (width, width),
        (width, width),
        (width, hidden_width),
        (width, hidden_width),
        (hidden_width, width),
    ]
    sizes_flat = [rows * cols // devices for rows, cols in shapes]
    slot_size = max(sizes_flat)
    whole_qkv, whole_out, whole_inner, whole_down = (
        lax.all_gather(qkv_next.astype(jnp.bfloat16), "dp", axis=1, tiled=True).astype(
            qkv_next.dtype
        ),
        lax.all_gather(out_next.astype(jnp.bfloat16), "dp", axis=0, tiled=True).astype(
            out_next.dtype
        ),
        lax.all_gather(inner_next.astype(jnp.bfloat16), "dp", axis=1, tiled=True).astype(
            inner_next.dtype
        ),
        lax.all_gather(down_next.astype(jnp.bfloat16), "dp", axis=0, tiled=True).astype(
            down_next.dtype
        ),
    )
    matrices = [
        whole_qkv[0],
        whole_qkv[1],
        whole_qkv[2],
        whole_out,
        whole_inner[0],
        whole_inner[1],
        whole_down,
    ]
    selected = jnp.zeros((width, hidden_width), jnp.float32)
    for index in range(7):
        selected = jnp.where(
            device_index == index * spacing,
            to_common(matrices[index], width, hidden_width),
            selected,
        )
    result = orthogonalize(selected)
    outgoing_rows = jnp.zeros((devices, slot_size), jnp.float32)
    for index in range(7):
        owned = jnp.where(device_index == index * spacing, from_common(result, shapes[index]), 0.0)
        pieces = owned.reshape(devices, sizes_flat[index])
        outgoing_rows = outgoing_rows + jnp.pad(
            pieces, ((0, 0), (0, slot_size - sizes_flat[index]))
        )
    incoming_rows = lax.all_to_all(
        outgoing_rows.astype(jnp.bfloat16), "dp", split_axis=0, concat_axis=0, tiled=True
    ).astype(outgoing_rows.dtype)
    shares = []
    for index in range(7):
        rows, cols = shapes[index]
        shares.append(
            incoming_rows[index * spacing, : sizes_flat[index]].reshape(rows // devices, cols)
        )
    qkv_update = jnp.stack(shares[0:3])
    out_update = shares[3]
    inner_update = jnp.stack(shares[4:6])
    down_update = shares[6]
    qkv_new = apply_step(qkv_weight, qkv_update, width, width)
    out_new = apply_step(out_weight, out_update, width, width)
    inner_new = apply_step(inner_weight, inner_update, width, hidden_width)
    down_new = apply_step(down_weight, down_update, hidden_width, width)
    gain_next = GAIN_MOMENTUM * gain_moment + gain_sum
    gains_new = gains - GAIN_RATE * gain_next
    return (
        block_output,
        input_grad,
        gain_sum,
        gain_next,
        gains_new,
        qkv_sum,
        out_sum,
        inner_sum,
        down_sum,
        qkv_new,
        out_new,
        inner_new,
        down_new,
        qkv_next,
        out_next,
        inner_next,
        down_next,
    )


def solution(mesh):
    in_specs = (
        P("dp", None),
        P("dp", None),
        P("dp", None),
        P(None, "dp"),
        P(None, "dp"),
        P(None, "dp", None),
        P("dp", None),
        P(None, "dp", None),
        P("dp", None),
        P(None, "dp", None),
        P("dp", None),
        P(None, "dp", None),
        P("dp", None),
    )
    out_specs = (
        P("dp", None),
        P("dp", None),
        P(None, "dp"),
        P(None, "dp"),
        P(None, "dp"),
        P(None, "dp", None),
        P("dp", None),
        P(None, "dp", None),
        P("dp", None),
        P(None, "dp", None),
        P("dp", None),
        P(None, "dp", None),
        P("dp", None),
        P(None, "dp", None),
        P("dp", None),
        P(None, "dp", None),
        P("dp", None),
    )
    return jax.shard_map(
        per_device, mesh=mesh, in_specs=in_specs, out_specs=out_specs, check_vma=False
    )
```

profile of v0, /device:TPU:0, one launch (start us, length us, event | category | flops | bytes accessed | tf_op | source)
XLA Modules:
  0.0 1511.8 jit_solution(13931384197841731313)
XLA Ops:
  14.2 33.1 %all-gather = bf16[128,6,2]{1,2,0:T(2,128)(2,1)S(1)} all-gather(bf16[1,6,2]{1,2,0:T(2,128)(2,1)S(1)} %convert_bitcast_fusion.2), channel_id=1, replica_groups=mesh['dp'=128] {'dp'}, dimensions={0}, use_global_device_ids=true | all-gather | bytes 3096 | tf_op jit(solution)/shard_map/all_gather | solution.py:144
  51.5 26.5 %all-gather.24.cloned.1.call-done = bf16[128,6,768]{2,1,0:T(8,128)(2,1)} async-done(((bf16[1,6,768]{2,1,0:T(8,128)(2,1)}), bf16[128,6,768]{2,1,0:T(8,128)(2,1)}) %all-gather.24.cloned.1.call-update) | async-done | bytes 1179664 | tf_op jit(solution)/shard_map/all_gather | solution.py:141
  81.3 64.9 %all-gather.12.cloned.1.call-done = bf16[3,768,768]{2,0,1:T(4,128)(2,1)} async-done(((bf16[3,6,768]{2,0,1:T(4,128)(2,1)}), bf16[3,768,768]{2,0,1:T(4,128)(2,1)}) %all-gather.12.cloned.1.call-update) | async-done | bytes 3538960 | tf_op jit(solution)/shard_map/all_gather | solution.py:140
  146.2 12.2 fusion.90
  160.4 6.5 copy.188
  166.9 4.4 copy.189
  176.6 41.6 %all-gather.14.cloned.1.call-done = bf16[2,768,3072]{2,0,1:T(2,128)(2,1)} async-done(((bf16[2,6,3072]{2,0,1:T(2,128)(2,1)}), bf16[2,768,3072]{2,0,1:T(2,128)(2,1)}) %all-gather.14.cloned.1.call-update) | async-done | bytes 9437200 | tf_op jit(solution)/shard_map/all_gather | solution.py:142
  218.3 19.0 %fusion.89 = (bf16[1,768,3072]{2,0,1:T(2,128)(2,1)S(1)}, bf16[1,768,3072]{2,0,1:T(2,128)(2,1)S(1)}) fusion(bf16[2,768,3072]{2,0,1:T(2,128)(2,1)} %all-gather.14.cloned.1.call-done), kind=kLoop, calls=%fused_computation.196 | loop fusion | bytes 18874368 | tf_op jit(solution)/shard_map/slice | solution.py:184
  247.1 39.3 %all-gather.16.cloned.1.call-done = bf16[3072,768]{1,0:T(8,128)(2,1)} async-done(((bf16[24,768]{1,0:T(8,128)(2,1)}), bf16[3072,768]{1,0:T(8,128)(2,1)}) %all-gather.16.cloned.1.call-update) | async-done | bytes 4718608 | tf_op jit(solution)/shard_map/all_gather | solution.py:143
  286.3 6.1 multiply_convert_fusion
  293.4 5.5 fusion.13
  310.6 5.1 convolution_bitcast_fusion.1
  322.0 5.0 pad_maximum_fusion
  327.0 37.0 %copy.157 = f32[2,768,3072]{2,0,1:T(2,128)} copy(f32[2,768,3072]{2,1,0:T(8,128)S(1)} %pad_maximum_fusion) | data formatting | bytes 37748736 | tf_op jit(solution)/shard_map/stack | solution.py:203
  364.0 6.5 pad_maximum_fusion.1
  371.6 5.3 fusion.93
  377.5 337.5 %fusion = f32[8,768]{1,0:T(8,128)S(1)} fusion(f32[768,768]{1,0:T(8,128)S(1)} %fusion.58), kind=kCustom, calls=%all-reduce-scatter | all-reduce-scatter fusion | flops 786433 | bytes 2383872
  726.8 11.9 collective-permute-start.22
  764.6 5.0 collective-permute-start.11
  777.3 4.3 collective-permute-start.6
  785.4 5.0 collective-permute-start.3
  804.6 21.5 %reduce-scatter.8.cloned.1.call-done = f32[24,768]{1,0:T(8,128)} async-done(((f32[3072,768]{1,0:T(8,128)}), f32[24,768]{1,0:T(8,128)}) %reduce-scatter.8.cloned.1.call-update) | async-done | bytes 73744
  830.6 60.8 %all-gather.26.cloned.1.call-done = bf16[128,6,768]{2,1,0:T(8,128)(2,1)} async-done(((bf16[1,6,768]{2,1,0:T(8,128)(2,1)}), bf16[128,6,768]{2,1,0:T(8,128)(2,1)}) %all-gather.26.cloned.1.call-update) | async-done | bytes 1179664 | tf_op jit(solution)/shard_map/all_gather | solution.py:299
  894.8 65.2 %all-gather.22.cloned.1.call-done = bf16[3,768,768]{2,0,1:T(4,128)(2,1)} async-done(((bf16[3,6,768]{2,0,1:T(4,128)(2,1)}), bf16[3,768,768]{2,0,1:T(4,128)(2,1)}) %all-gather.22.cloned.1.call-update) | async-done | bytes 3538960 | tf_op jit(solution)/shard_map/all_gather | solution.py:296
  965.5 63.1 %all-gather.18.cloned.1.call-done = bf16[3072,768]{1,0:T(8,128)(2,1)} async-done(((bf16[24,768]{1,0:T(8,128)(2,1)}), bf16[3072,768]{1,0:T(8,128)(2,1)}) %all-gather.18.cloned.1.call-update) | async-done | bytes 4718608 | tf_op jit(solution)/shard_map/all_gather | solution.py:305
  1028.6 6.6 copy.161
  1035.2 65.7 %all-gather.20.cloned.1.call-done = bf16[2,768,3072]{2,0,1:T(2,128)(2,1)} async-done(((bf16[2,6,3072]{2,0,1:T(2,128)(2,1)}), bf16[2,768,3072]{2,0,1:T(2,128)(2,1)}) %all-gather.20.cloned.1.call-update) | async-done | bytes 9437200 | tf_op jit(solution)/shard_map/all_gather | solution.py:302
  1100.9 13.6 copy_convert_fusion
  1114.5 15.1 multiply_reduce_fusion
  1130.3 27.2 %fusion.6 = f32[768,768]{1,0:T(8,128)S(1)} fusion(f32[768,3072]{1,0:T(8,128)} %get-tuple-element.204, f32[]{:T(128)S(6)} %add.174), kind=kOutput, calls=%fused_computation.23 | convolution fusion | flops 21745631232 | bytes 11796484 | tf_op jit(solution)/shard_map/dot_general | solution.py:88
  1157.5 6.0 fusion.94
  1163.5 24.2 %multiply_add_fusion.1 = f32[768,3072]{1,0:T(8,128)S(1)} fusion(f32[768,3072]{1,0:T(8,128)S(1)} %copy-done.10, f32[]{:T(128)S(6)} %add.174, f32[768,768]{1,0:T(8,128)S(1)} %fusion.94, f32[768,768]{1,0:T(8,128)S(1)} %fusion.6), kind=kOutput, calls=%fused_computation.12 | convolution fusion | flops 21754478592 | bytes 23592964 | tf_op jit(solution)/shard_map/dot_general | solution.py:92
  1187.7 24.1 %fusion.95 = f32[768,768]{1,0:T(8,128)S(1)} fusion(f32[768,3072]{1,0:T(8,128)S(1)} %multiply_add_fusion.1), kind=kOutput, calls=%fused_computation.202 | convolution fusion | flops 21743271936 | bytes 11796480 | tf_op jit(solution)/shard_map/dot_general | solution.py:88
  1211.8 6.0 fusion.96
  1217.8 24.1 %multiply_add_fusion = f32[768,3072]{1,0:T(8,128)S(1)} fusion(f32[768,3072]{1,0:T(8,128)S(1)} %multiply_add_fusion.1, f32[768,768]{1,0:T(8,128)S(1)} %fusion.96, f32[768,768]{1,0:T(8,128)S(1)} %fusion.95), kind=kOutput, calls=%fused_computation.11 | convolution fusion | flops 21749760000 | bytes 23592960 | tf_op jit(solution)/shard_map/dot_general | solution.py:92
  1241.9 9.8 broadcast_select_fusion.1
  1254.8 9.6 copy.165
  1264.4 10.0 reshape.309
  1274.4 11.3 reshape.308
  1285.7 11.3 reshape.307
  1307.8 14.7 fusion.5
  1323.0 7.3 reduce.24
  1330.3 8.2 reshape.348
  1338.5 6.7 all-to-all-start
  1350.8 103.3 %all-reduce.8 = f32[2,768]{1,0:T(2,128)S(1)} all-reduce(f32[2,768]{1,0:T(2,128)S(1)} %pad_maximum_fusion.8), channel_id=2, replica_groups=mesh['dp'=128] {'dp'}, use_global_device_ids=true, to_apply=%region_12.13.clone | all-reduce | flops 1536 | bytes 12288
  1461.8 19.9 %reshape.349 = bf16[128,1,18432]{2,1,0:T(2,128)(2,1)} reshape(bf16[128,2,9216]{2,1,0:T(2,128)(2,1)} %all-to-all-done) | data formatting | bytes 9437184
  1481.7 7.0 copy.217
  1488.8 11.1 convert_element_type.209
  (277 shorter events, 160.1 us)
Async XLA Ops:
  7.2 70.9 %all-gather.24.cloned.1.call-start = ((), (), s32[]{:S(2)}) async-start(), calls=%async_computation.8 | async-start | bytes 1585152 | tf_op jit(solution)/shard_map/all_gather | solution.py:141
  8.6 137.6 %all-gather.12.cloned.1.call-start = ((), (), s32[]{:S(2)}) async-start(), calls=%async_computation.2 | async-start | bytes 4755456 | tf_op jit(solution)/shard_map/all_gather | solution.py:140
  10.2 208.1 %all-gather.14.cloned.1.call-start = ((), (), s32[]{:S(2)}) async-start(), calls=%async_computation.3 | async-start | bytes 9510912 | tf_op jit(solution)/shard_map/all_gather | solution.py:142
  11.9 274.4 %all-gather.16.cloned.1.call-start = ((), (), s32[]{:S(2)}) async-start(), calls=%async_computation.4 | async-start | bytes 4755456 | tf_op jit(solution)/shard_map/all_gather | solution.py:143
  13.5 788.6 %all-reduce.16.cloned.1.call-start = ((), (), s32[]{:S(2)}) async-start(), calls=%async_computation.11 | async-start | bytes 51904512
  48.3 271.7 %copy-start.34 = (f32[768]{0:T(1024)}, f32[768]{0:T(1024)S(1)}, u32[]{:S(2)}) copy-start(f32[768]{0:T(1024)S(1)} %get-tuple-element.200) | copy-start | bytes 9220
  370.5 455.6 %reduce-scatter.8.cloned.1.call-start = ((), (), s32[]{:S(2)}) async-start(), calls=%async_computation.10 | async-start | bytes 9510912
  376.9 424.4 %copy-start.46 = (f32[6,768]{1,0:T(8,128)S(1)}, f32[6,768]{1,0:T(8,128)}, u32[]{:S(2)}) copy-start(f32[6,768]{1,0:T(8,128)} %param.23) | copy-start | bytes 55300
  377.0 425.2 %copy-start.44 = (f32[3,6,768]{2,1,0:T(8,128)S(1)}, f32[3,6,768]{2,1,0:T(8,128)}, u32[]{:S(2)}) copy-start(f32[3,6,768]{2,1,0:T(8,128)} %param.22) | copy-start | bytes 165892
  377.0 427.5 %copy-start.43 = (f32[24,768]{1,0:T(8,128)S(1)}, f32[24,768]{1,0:T(8,128)}, u32[]{:S(2)}) copy-start(f32[24,768]{1,0:T(8,128)} %param.25) | copy-start | bytes 221188
  377.0 451.8 %copy-start.38 = (f32[2,6,3072]{2,0,1:T(2,128)S(1)}, f32[2,6,3072]{2,0,1:T(2,128)}, u32[]{:S(2)}) copy-start(f32[2,6,3072]{2,0,1:T(2,128)} %param.24) | copy-start | bytes 442372
  377.0 514.4 %all-gather.26.cloned.1.call-start = ((), (), s32[]{:S(2)}) async-start(), calls=%async_computation.9 | async-start | bytes 1585152 | tf_op jit(solution)/shard_map/all_gather | solution.py:299
  715.0 7.8 collective-permute-start.30
  716.3 5.2 collective-permute-start.31
  717.6 6.5 collective-permute-start.29
  718.9 6.5 collective-permute-start.28
  720.2 6.5 collective-permute-start.27
  721.6 17.1 %collective-permute-start.26 = (f32[8,768]{1,0:T(8,128)S(1)}, f32[8,768]{1,0:T(8,128)S(1)}, u32[]{:S(2)}, u32[]{:S(2)}) collective-permute-start(f32[8,768]{1,0:T(8,128)S(1)} %fusion), channel_id=1, source_target_pairs={{0,27},{1,28},{2,29},{3,30},{4,31},{5,32},{6,33},{7,34},{8,35},{9,... | collective-permute-start | bytes 73736
  722.9 19.9 %collective-permute-start.25 = (f32[8,768]{1,0:T(8,128)S(1)}, f32[8,768]{1,0:T(8,128)S(1)}, u32[]{:S(2)}, u32[]{:S(2)}) collective-permute-start(f32[8,768]{1,0:T(8,128)S(1)} %fusion), channel_id=1, source_target_pairs={{0,26},{1,27},{2,28},{3,29},{4,30},{5,31},{6,32},{7,33},{8,34},{9,... | collective-permute-start | bytes 73736
  724.2 20.5 %collective-permute-start.24 = (f32[8,768]{1,0:T(8,128)S(1)}, f32[8,768]{1,0:T(8,128)S(1)}, u32[]{:S(2)}, u32[]{:S(2)}) collective-permute-start(f32[8,768]{1,0:T(8,128)S(1)} %fusion), channel_id=1, source_target_pairs={{0,25},{1,26},{2,27},{3,28},{4,29},{5,30},{6,31},{7,32},{8,33},{9,... | collective-permute-start | bytes 73736
  725.5 23.0 %collective-permute-start.23 = (f32[8,768]{1,0:T(8,128)S(1)}, f32[8,768]{1,0:T(8,128)S(1)}, u32[]{:S(2)}, u32[]{:S(2)}) collective-permute-start(f32[8,768]{1,0:T(8,128)S(1)} %fusion), channel_id=1, source_target_pairs={{0,24},{1,25},{2,26},{3,27},{4,28},{5,29},{6,30},{7,31},{8,32},{9,... | collective-permute-start | bytes 73736
  726.8 23.0 %collective-permute-start.22 = (f32[8,768]{1,0:T(8,128)S(1)}, f32[8,768]{1,0:T(8,128)S(1)}, u32[]{:S(2)}, u32[]{:S(2)}) collective-permute-start(f32[8,768]{1,0:T(8,128)S(1)} %fusion), channel_id=1, source_target_pairs={{0,23},{1,24},{2,25},{3,26},{4,27},{5,28},{6,29},{7,30},{8,31},{9,... | collective-permute-start | bytes 73736
  738.7 13.9 collective-permute-start.21
  742.8 12.7 collective-permute-start.20
  744.7 12.0 collective-permute-start.19
  748.4 10.2 collective-permute-start.18
  749.7 12.0 collective-permute-start.17
  752.6 12.1 collective-permute-start.16
  755.4 14.2 collective-permute-start.15
  756.7 14.2 collective-permute-start.14
  758.7 13.6 collective-permute-start.13
  761.8 13.3 collective-permute-start.12
  764.6 12.7 collective-permute-start.11
  769.6 12.0 collective-permute-start.10
  770.9 12.3 collective-permute-start.9
  772.2 13.2 collective-permute-start.8
  775.1 15.3 %collective-permute-start.7 = (f32[8,768]{1,0:T(8,128)S(1)}, f32[8,768]{1,0:T(8,128)S(1)}, u32[]{:S(2)}, u32[]{:S(2)}) collective-permute-start(f32[8,768]{1,0:T(8,128)S(1)} %fusion), channel_id=1, source_target_pairs={{0,8},{1,9},{2,10},{3,11},{4,12},{5,13},{6,14},{7,15},{8,16},{9,17... | collective-permute-start | bytes 73736
  777.3 14.4 collective-permute-start.6
  781.6 13.1 collective-permute-start.5
  783.2 13.9 collective-permute-start.4
  785.4 11.8 collective-permute-start.3
  790.4 6.8 collective-permute-start.2
  791.7 5.5 collective-permute-start.1
  794.8 3.2 collective-permute-start
  802.0 158.0 %all-gather.22.cloned.1.call-start = ((), (), s32[]{:S(2)}) async-start(), calls=%async_computation.7 | async-start | bytes 4755456 | tf_op jit(solution)/shard_map/all_gather | solution.py:296
  804.4 224.2 %all-gather.18.cloned.1.call-start = ((), (), s32[]{:S(2)}) async-start(), calls=%async_computation.5 | async-start | bytes 4755456 | tf_op jit(solution)/shard_map/all_gather | solution.py:305
  828.7 272.2 %all-gather.20.cloned.1.call-start = ((), (), s32[]{:S(2)}) async-start(), calls=%async_computation.6 | async-start | bytes 9510912 | tf_op jit(solution)/shard_map/all_gather | solution.py:302
  1338.5 123.2 %all-to-all-start = ((bf16[128,2,9216]{2,1,0:T(2,128)(2,1)}), bf16[128,2,9216]{2,1,0:T(2,128)(2,1)}, u32[]{:S(2)}, u32[]{:S(2)}) async-start(bf16[128,2,9216]{2,1,0:T(2,128)(2,1)} %reshape.348), calls=%async_computation | async-start | bytes 9437184 | tf_op jit(solution)/shard_map/all_to_all | solution.py:333
  (46 other events, 1449.3 us)
Sparse Core Ops, SparseCore 0:
  11.4 66.6 all-gather.23
  81.7 64.4 all-gather.11
  149.8 68.3 all-gather.13
  221.7 64.5 all-gather.15
  370.6 231.8 all-reduce.15
  608.8 217.2 reduce-scatter.7
  829.8 61.5 all-gather.25
  895.5 64.4 all-gather.21
  964.0 64.5 all-gather.17
  1032.5 68.3 all-gather.19
where the time goes:
time: 1520 us; the launch traced here: 1510 us
  blocking collectives  474 us (31%)
  waiting for transfers between devices  450 us (30%)
  local copies, waits for them, and re-layouts  200 us (13%)
  matrix products  172 us (11%)
  other arithmetic  110 us (7%)
  starting transfers between devices  88.7 us (6%)
  between operations  16.8 us (1%)
    unnamed x2, blocking collectives  441 us
    unnamed x34, starting transfers between devices  81.7 us
    all_gather x1, waiting for transfers between devices, per_device(): lax.all_gather(inner_next.astype(jnp.bfloat16), 'dp', axis=1, tiled=True)  65.7 us
    all_gather x1, waiting for transfers between devices, per_device(): lax.all_gather(qkv_next.astype(jnp.bfloat16), 'dp', axis=1, tiled=True)  65.2 us
    all_gather x1, waiting for transfers between devices, per_device(): lax.all_gather(qkv_weight.astype(jnp.bfloat16), 'dp', axis=1, tiled=True)  64.9 us
    all_gather x1, waiting for transfers between devices, per_device(): lax.all_gather(down_next.astype(jnp.bfloat16), 'dp', axis=0, tiled=True)  63.1 us
    all_gather x1, waiting for transfers between devices, per_device(): lax.all_gather(out_next.astype(jnp.bfloat16), 'dp', axis=0, tiled=True)  60.8 us
    unnamed x115, local copies, waits for them, and re-layouts  56.8 us
  transfers between devices with their start and end apart: 43, of which 10 were waited for; matrix products, arithmetic and copies ran while one was open for 30% of the time, Pallas kernels for 0%

commit v1 on v0

v1 whole, which is shorter than its diff:
```python
import math

import jax
import jax.numpy as jnp
import numpy as np
from jax import lax
from jax.sharding import Mesh
from jax.sharding import PartitionSpec as P

HEAD = 64
HALF = 384
WIDTH = 768
PACK = 128
EPSILON = 1e-06
ROPE_BASE = 10000.0
MOMENTUM = 0.95
GAIN_MOMENTUM = 0.9
MUON_RATE = 0.3
GAIN_RATE = 0.001
WEIGHT_DECAY = 0.1
POLY_LINEAR = 3.4445
POLY_CUBIC = -4.775
POLY_QUINTIC = 2.0315

AXES = ("z", "y", "x", "c")
SWAP = [(0, 1), (1, 0)]
BF = jnp.bfloat16
F32 = jnp.float32


def mm(left, right):
    return jnp.dot(left, right, preferred_element_type=F32)


def mm_nt(left, right):
    return lax.dot_general(left, right, (((1,), (1,)), ((), ())), preferred_element_type=F32)


def mm_tn(left, right):
    return lax.dot_general(left, right, (((0,), (0,)), ((), ())), preferred_element_type=F32)


def swap_core(value):
    return lax.ppermute(value, "c", SWAP)


def by_core(core, own, other):
    return jnp.where(core == 0, jnp.stack([own, other]), jnp.stack([other, own]))


def shift(axis, step):
    return [(i, (i + step) % 4) for i in range(4)]


def scatter_sum(chunks, axis):
    me = lax.axis_index(axis)
    total = lax.dynamic_index_in_dim(chunks, me, 0, keepdims=False).astype(F32)
    for step in (1, 3, 2):
        piece = lax.dynamic_index_in_dim(chunks, (me + step) % 4, 0, keepdims=False)
        total = total + lax.ppermute(piece, axis, shift(axis, step)).astype(F32)
    return total


def gather_four(value, axis):
    me = lax.axis_index(axis)
    full = jnp.zeros((4,) + value.shape, value.dtype)
    full = lax.dynamic_update_index_in_dim(full, value, me, 0)
    for step in (1, 3, 2):
        got = lax.ppermute(value, axis, shift(axis, step))
        full = lax.dynamic_update_index_in_dim(full, got, (me + 4 - step) % 4, 0)
    return full


def gather_xc(value, core):
    line = gather_four(value, "x")
    both = by_core(core, line, swap_core(line))
    return jnp.moveaxis(both, 0, 1).reshape((8 * value.shape[0],) + value.shape[1:])


def exchange(value, axis):
    return lax.all_to_all(value, axis, split_axis=0, concat_axis=0, tiled=True)


def one_hot(order):
    table = np.zeros((len(order), len(order)), np.float32)
    table[np.asarray(order), np.arange(len(order))] = 1.0
    return jnp.asarray(table, BF)


def norm_order():
    grid = np.arange(WIDTH).reshape(4, 4, 4, 2, 6)
    return grid.transpose(2, 3, 1, 0, 4).reshape(-1)


def out_order():
    grid = np.arange(HALF).reshape(2, 4, 4, 2, 6)
    return grid.transpose(2, 3, 1, 0, 4).reshape(-1)


def down_order():
    grid = np.arange(HALF).reshape(2, 4, 2, 24)
    return grid.transpose(1, 2, 0, 3).reshape(-1)


def segment_table(lengths, count):
    ends = jnp.cumsum(lengths, dtype=jnp.int32)
    places = jnp.arange(count, dtype=jnp.int32)
    segment = jnp.sum((places[:, None] >= ends[None, :]).astype(jnp.int32), axis=1, dtype=jnp.int32)
    starts = ends - lengths
    slots = jnp.arange(lengths.shape[0], dtype=jnp.int32)
    first = jnp.sum(
        jnp.where(segment[:, None] == slots[None, :], starts[None, :], 0), axis=1, dtype=jnp.int32
    )
    return (segment, places - first)


def rotate(values, cosine, sine):
    half = values.shape[-1] // 2
    first = values[..., :half]
    second = values[..., half:]
    return jnp.concatenate(
        [first * cosine - second * sine, second * cosine + first * sine], axis=-1
    )


def norm_scale(values):
    return lax.rsqrt(jnp.mean(values * values, axis=-1, keepdims=True) + EPSILON)


def norm_backward(values, scale, gain, grad):
    scaled = grad * gain
    return scale * scaled - values * (scale * scale * scale) * jnp.mean(
        scaled * values, axis=-1, keepdims=True
    )


def to_units(qkv, out, inner, down):
    first = jnp.concatenate([qkv, out[None]])
    wide = inner.reshape(2, 6, 4, WIDTH).transpose(0, 2, 1, 3)
    pieces = jnp.concatenate([first[None], wide, down.reshape(1, 4, 6, WIDTH)])
    got = exchange(pieces, "z")
    turned = jnp.where(lax.axis_index("z") == 3, got, got.transpose(1, 0, 2, 3))
    return exchange(turned, "y").reshape(96, WIDTH)


def to_owners(rows):
    got = exchange(rows.reshape(4, 4, 6, WIDTH), "y")
    turned = jnp.where(lax.axis_index("z") == 3, got, got.transpose(1, 0, 2, 3))
    back = exchange(turned, "z")
    inner = back[1:3].transpose(0, 2, 1, 3).reshape(2, 6, 4 * WIDTH)
    return back[0, :3], back[0, 3], inner, back[3].reshape(24, WIDTH)


def per_device(
    tokens,
    cotangent,
    lengths,
    gains,
    gain_moment,
    qkv_weight,
    out_weight,
    inner_weight,
    down_weight,
    qkv_moment,
    out_moment,
    inner_moment,
    down_moment,
):
    z, y, x, core = (lax.axis_index(name) for name in AXES)
    first = jnp.concatenate([qkv_weight, out_weight[None]]).astype(BF)
    first = first.reshape(4, 6, 2, HALF).transpose(0, 2, 1, 3)
    wide = inner_weight.astype(BF).reshape(2, 6, 4, 2, HALF).transpose(0, 2, 3, 1, 4)
    blocks = jnp.stack([first, wide[0], wide[1]], axis=2).reshape(8, 3, 6, HALF)
    blocks = exchange(blocks, ("x", "c")).transpose(1, 0, 2, 3).reshape(144, HALF)
    down_piece = down_weight.astype(BF).reshape(24, 2, HALF).transpose(1, 0, 2).reshape(48, HALF)
    gain_piece = jnp.pad(gains.astype(BF), ((0, 14), (0, HALF - 6)))
    piece = jnp.concatenate([blocks, down_piece, gain_piece])
    whole = lax.all_gather(piece, AXES, axis=0, tiled=False)
    tokens2 = by_core(core, tokens, swap_core(tokens)).reshape(2 * PACK, WIDTH)
    cot2 = by_core(core, cotangent, swap_core(cotangent)).reshape(2 * PACK, WIDTH)
    lengths2 = by_core(core, lengths[0], swap_core(lengths[0].astype(F32)).astype(jnp.int32))
    moment_rows = to_units(qkv_moment, out_moment, inner_moment, down_moment)
    segment, position = jax.vmap(lambda row: segment_table(row, PACK))(lengths2)
    freq = ROPE_BASE ** (-jnp.arange(HEAD // 2, dtype=F32) / (HEAD // 2))
    angle = position.astype(F32)[:, :, None] * freq
    cosine = jnp.cos(angle)[:, :, None, :]
    sine = jnp.sin(angle)[:, :, None, :]
    places = jnp.arange(PACK, dtype=jnp.int32)
    allowed = (segment[:, :, None] == segment[:, None, :]) & (places[None, :] <= places[:, None])
    allowed = allowed[:, None]
    inputs = tokens2.astype(F32)
    scale_one = norm_scale(inputs)

    grid = whole.reshape(16, 4, 2, 208, HALF)
    gains_full = (
        whole[:, 192:194, :6].transpose(1, 0, 2).reshape(2, WIDTH).astype(F32)
    )
    mine = lax.dynamic_index_in_dim(grid, core, 2, keepdims=False)
    qkv_c = mine[:, :3, 0:48].transpose(1, 0, 2, 3).reshape(3, WIDTH, HALF)
    out_full = grid[:, 3, :, 0:48].transpose(0, 2, 1, 3).reshape(WIDTH, WIDTH)
    gate_c = mine[:, :, 48:96].transpose(0, 2, 1, 3).reshape(WIDTH, 4 * HALF)
    up_c = mine[:, :, 96:144].transpose(0, 2, 1, 3).reshape(WIDTH, 4 * HALF)
    down_c = lax.dynamic_index_in_dim(
        whole.reshape(4, 2, 16, 208, HALF), core, 1, keepdims=False
    )[:, :, 144:192]
    down_c = down_c.reshape(4, 16, 2, 24, HALF).transpose(0, 1, 3, 2, 4).reshape(4 * HALF, WIDTH)

    normed = (inputs * scale_one * gains_full[0]).astype(BF)
    heads = HALF // HEAD
    by_head = (2, PACK, heads, HEAD)
    query = rotate(mm(normed, qkv_c[0]).reshape(by_head), cosine, sine).astype(BF)
    keys = rotate(mm(normed, qkv_c[1]).reshape(by_head), cosine, sine).astype(BF)
    values = mm(normed, qkv_c[2]).astype(BF).reshape(by_head)
    dots = jnp.einsum("pqhd,pkhd->phqk", query, keys, preferred_element_type=F32) * HEAD**-0.5
    dots = jnp.where(allowed, dots, -1e30)
    top = jnp.max(dots, axis=-1, keepdims=True)
    weights = jnp.exp(dots - top)
    total = jnp.sum(weights, axis=-1, keepdims=True)
    probs = weights / total
    probs_low = probs.astype(BF)
    mixed_c = jnp.einsum("phqk,pkhd->pqhd", probs_low, values, preferred_element_type=F32)
    mixed_c = mixed_c.astype(BF).reshape(2 * PACK, HALF)
    both = by_core(core, mixed_c, swap_core(mixed_c))
    mixed = jnp.concatenate([both[0], both[1]], axis=1)
    middle = inputs + mm(mixed, out_full)
    scale_two = norm_scale(middle)
    normed_two = (middle * scale_two * gains_full[1]).astype(BF)
    gate = mm(normed_two, gate_c)
    upward = mm(normed_two, up_c)
    sigma = jax.nn.sigmoid(gate)
    activated = gate * sigma
    hidden = (activated * upward).astype(BF)

    def own_pack(value):
        return lax.dynamic_slice_in_dim(value, core * PACK, PACK, 0)

    def other_pack(value):
        return lax.dynamic_slice_in_dim(value, (1 - core) * PACK, PACK, 0)

    down_order_hot = one_hot(down_order())
    hidden_turned = mm(hidden.reshape(-1, HALF), down_order_hot).astype(BF).reshape(2 * PACK, 4 * HALF)
    down_grad = mm_tn(hidden_turned, cot2).astype(BF)
    down_chunks = (
        down_grad.reshape(4, 8, 48, 2, HALF).transpose(0, 1, 3, 2, 4).reshape(4, 4, 192, HALF)
    )
    hidden_grad = mm_nt(cot2, down_c)
    gate_grad = (hidden_grad * upward * (sigma * (1.0 + gate * (1.0 - sigma)))).astype(BF)
    up_grad = (hidden_grad * activated).astype(BF)
    turn = one_hot(norm_order())
    two_turned = mm(normed_two, turn).astype(BF)

    def column_chunks(rows, grad):
        part = mm_tn(rows, grad).astype(BF)
        blocks_of = part.shape[1] // HALF
        return part.reshape(4, 192, blocks_of, HALF).transpose(2, 0, 1, 3)

    gate_chunks = column_chunks(two_turned, gate_grad)
    up_chunks = column_chunks(two_turned, up_grad)
    two_part = mm_nt(gate_grad, gate_c) + mm_nt(up_grad, up_c)
    normed_two_grad = two_part + swap_core(two_part)
    middle_grad = cot2.astype(F32) + norm_backward(
        middle, scale_two, gains_full[1], normed_two_grad
    )
    branch_grad = middle_grad.astype(BF)
    down_part = mm(hidden, down_c)
    block_output = (
        own_pack(middle) + own_pack(down_part) + swap_core(other_pack(down_part))
    ).astype(BF)

    def rows_first(chunks):
        return scatter_sum(jnp.swapaxes(chunks, 0, 1), "x").astype(BF)

    def units_first(chunks):
        return scatter_sum(chunks, "y").astype(BF)

    down_rows = rows_first(down_chunks)
    up_rows = units_first(up_chunks)
    gate_rows = rows_first(gate_chunks)

    out_turned = mm(mixed_c, one_hot(out_order())).astype(BF)
    out_grad = mm_tn(out_turned, branch_grad).astype(BF)
    out_chunk = out_grad.reshape(8, 48, 2, HALF).transpose(0, 2, 1, 3).reshape(4, 192, HALF)
    out_rows = lax.dynamic_slice_in_dim(out_full, core * HALF, HALF, 0)
    mixed_grad = mm_nt(branch_grad, out_rows).astype(BF).reshape(by_head)
    values_grad = jnp.einsum("phqk,pqhd->pkhd", probs_low, mixed_grad, preferred_element_type=F32)
    probs_grad = jnp.einsum("pqhd,pkhd->phqk", mixed_grad, values, preferred_element_type=F32)
    centre = jnp.sum(probs * probs_grad, axis=-1, keepdims=True)
    dots_grad = (probs * (probs_grad - centre) * HEAD**-0.5).astype(BF)
    query_grad = jnp.einsum("phqk,pkhd->pqhd", dots_grad, keys, preferred_element_type=F32)
    keys_grad = jnp.einsum("phqk,pqhd->pkhd", dots_grad, query, preferred_element_type=F32)
    flat = (2 * PACK, HALF)
    query_grad = rotate(query_grad, cosine, -sine).astype(BF).reshape(flat)
    keys_grad = rotate(keys_grad, cosine, -sine).astype(BF).reshape(flat)
    values_grad = values_grad.astype(BF).reshape(flat)
    one_turned = mm(normed, turn).astype(BF)
    qkv_chunks = column_chunks(
        one_turned, jnp.concatenate([query_grad, keys_grad, values_grad], axis=1)
    )
    one_part = (
        mm_nt(query_grad, qkv_c[0]) + mm_nt(keys_grad, qkv_c[1]) + mm_nt(values_grad, qkv_c[2])
    )
    normed_grad = own_pack(one_part) + swap_core(other_pack(one_part))
    own_inputs = own_pack(inputs)
    own_scale = own_pack(scale_one)
    input_grad = own_pack(middle_grad) + norm_backward(
        own_inputs, own_scale, gains_full[0], normed_grad
    )
    gain_local = jnp.stack(
        [
            jnp.sum(normed_grad * own_inputs * own_scale, axis=0),
            jnp.sum(own_pack(normed_two_grad * middle * scale_two), axis=0),
        ]
    )
    gain_rows = (
        gain_local.reshape(2, 4, 4, 4, 2, 6).transpose(2, 3, 0, 1, 4, 5).reshape(4, 4, 1, 96)
    )
    gain_rows = jnp.pad(gain_rows, ((0, 0), (0, 0), (0, 15), (0, HALF - 96))).astype(BF)
    first_chunks = jnp.concatenate([qkv_chunks, out_chunk[None]])
    first_chunks = jnp.concatenate([first_chunks, gain_rows], axis=2)
    first_rows = units_first(first_chunks)

    down_rows = units_first(down_rows)
    gate_rows = units_first(gate_rows)
    up_rows = scatter_sum(up_rows, "x").astype(BF)
    first_rows = scatter_sum(first_rows, "x").astype(BF)
    gain_part = first_rows[192, :96].reshape(2, 4, 12).transpose(1, 0, 2).reshape(4, 1, 24)
    gain_part = jnp.pad(gain_part, ((0, 0), (0, 15), (0, HALF - 24)))
    planes = jnp.stack([first_rows[:192], gate_rows, up_rows, down_rows])
    planes = jnp.concatenate([planes, gain_part], axis=1)
    summed = scatter_sum(planes, "z")

    rows = summed[:192].reshape(2, 96, HALF)
    keep = lax.dynamic_index_in_dim(rows, core, 0, keepdims=False)
    send = lax.dynamic_index_in_dim(rows, 1 - core, 0, keepdims=False)
    gain_sums = summed[192, :24].reshape(2, 2, 6).transpose(1, 0, 2)
    gain_keep = lax.dynamic_index_in_dim(gain_sums, core, 0, keepdims=False)
    gain_send = lax.dynamic_index_in_dim(gain_sums, 1 - core, 0, keepdims=False)
    gain_grad = gain_keep + swap_core(gain_send)
    halves = by_core(core, keep, swap_core(send))
    as_columns = jnp.concatenate([halves[0], halves[1]], axis=1)
    as_down = halves.reshape(2, 2, 48, HALF).transpose(0, 2, 1, 3).reshape(96, WIDTH)
    as_out = (
        halves.reshape(2, 2, 4, 12, HALF).transpose(2, 0, 3, 1, 4).reshape(96, WIDTH)
    )
    unit_grad = jnp.where(
        z == 3, as_down, jnp.where((z == 0) & (y == 3), as_out, as_columns)
    )

    moment_next = MOMENTUM * moment_rows + unit_grad
    own_rows = moment_next.astype(BF)
    unit = gather_xc(own_rows, core)
    tall = z == 3
    gram = jnp.where(tall, mm_tn(unit, unit), mm_nt(unit, unit))
    slot = 2 * x + core
    gram_rows = lax.dynamic_slice_in_dim(gram, slot * 96, 96, 0).astype(BF)
    gram_sum = gram_rows.astype(F32)
    for step in (1, 3, 2):
        gram_sum = gram_sum + lax.ppermute(gram_rows, "y", shift("y", step)).astype(F32)
    gram_rows = jnp.where(z == 0, gram_rows, gram_sum.astype(BF))
    gram = gather_xc(gram_rows, core)
    size = jnp.sqrt(jnp.sum(jnp.diagonal(gram).astype(F32))) + 1e-07
    scale = 1.0 / (size * size)
    square = gram.astype(F32) * scale
    low = square.astype(BF)
    square2 = mm(low, low)
    poly = POLY_CUBIC * square + POLY_QUINTIC * square2
    poly_low = poly.astype(BF)
    step_one = mm(low, poly_low)
    step_two = mm(step_one.astype(BF), poly_low)
    square = POLY_LINEAR**2 * square + 2.0 * POLY_LINEAR * step_one + step_two
    low = square.astype(BF)
    poly_next = POLY_CUBIC * square + POLY_QUINTIC * mm(low, low)
    factor = POLY_LINEAR * (poly + poly_next) + mm(poly_next.astype(BF), poly_low)
    factor = factor.astype(BF)
    factor_rows = lax.dynamic_slice_in_dim(factor, slot * 96, 96, 0)
    left = jnp.where(tall, own_rows, factor_rows)
    right = jnp.where(tall, factor, unit)
    result = (mm(left, right) + POLY_LINEAR**2 * own_rows.astype(F32)) / size

    qkv_sum, out_sum, inner_sum, down_sum = to_owners(unit_grad.astype(BF))
    qkv_turn, out_turn, inner_turn, down_turn = to_owners(result.astype(BF))
    sums = [value.astype(F32) for value in (qkv_sum, out_sum, inner_sum, down_sum)]
    moments = [
        MOMENTUM * old + new
        for old, new in zip((qkv_moment, out_moment, inner_moment, down_moment), sums)
    ]
    weights_new = [
        old * (1.0 - MUON_RATE * WEIGHT_DECAY)
        - MUON_RATE * (0.2 * math.sqrt(longest)) * turned.astype(F32)
        for old, turned, longest in (
            (qkv_weight, qkv_turn, WIDTH),
            (out_weight, out_turn, WIDTH),
            (inner_weight, inner_turn, 4 * WIDTH),
            (down_weight, down_turn, 4 * WIDTH),
        )
    ]
    gain_next = GAIN_MOMENTUM * gain_moment + gain_grad
    gains_new = gains - GAIN_RATE * gain_next
    return (
        block_output,
        input_grad,
        gain_grad,
        gain_next,
        gains_new,
        *sums,
        *weights_new,
        *moments,
    )


def solution(mesh):
    grid = Mesh(mesh.devices.reshape(4, 4, 4, 2), AXES)
    rows = P(AXES, None)
    middle = P(None, AXES)
    stacked = P(None, AXES, None)
    weights = (stacked, rows, stacked, rows)
    in_specs = (rows, rows, rows, middle, middle) + weights + weights
    out_specs = (rows, rows, middle, middle, middle) + weights * 3
    return jax.shard_map(
        per_device, mesh=grid, in_specs=in_specs, out_specs=out_specs, check_vma=False
    )
```

time: 1520 us -> 500 us (0.33)
  blocking collectives: 474 us -> 0 us
  waiting for transfers between devices: 450 us -> 164 us
  matrix products: 172 us -> 48.5 us
  local copies, waits for them, and re-layouts: 200 us -> 125 us
  other arithmetic: 110 us -> 53.5 us
    unnamed x2 -> x0, blocking collectives: 441 us -> none
    all_gather x8 -> x1, waiting for transfers between devices: 427 us -> 80 us  [per_device(): whole = lax.all_gather(piece, AXES, axis=0, tiled=False)]
    dot_general x32 -> x34, matrix products: 167 us -> 46.2 us  [the longest x15 15.9 us: mm(): return jnp.dot(left, right, preferred_element_type=F32)]
    unnamed x34 -> x0, starting transfers between devices: 81.7 us -> none
    ppermute x0 -> x47, starting transfers between devices: none -> 56.4 us  [the longest x27 41.1 us: scatter_sum(): total = total + lax.ppermute(piece, axis, shift(axis, step)).astype(F32)]
    ppermute x0 -> x47, waiting for transfers between devices: none -> 48.6 us  [the longest x27 28.4 us: scatter_sum(): total = total + lax.ppermute(piece, axis, shift(axis, step)).astype(F32)]
    unnamed x115 -> x202, local copies, waits for them, and re-layouts: 56.8 us -> 18.1 us
    all_to_all x1 -> x7, waiting for transfers between devices: 0.01 us -> 35.3 us  [exchange(): return lax.all_to_all(value, axis, split_axis=0, concat_axis=0, tiled=True)]
  transfers between devices with their start and end apart: 43 -> 55, of which waited for: 10 -> 32; matrix products, arithmetic and copies ran while one was open for 30% -> 25% of each run, Pallas kernels for 0% -> 0%
where the time goes in v1:
time: 500 us; the launch traced here: 491 us
  waiting for transfers between devices  164 us (33%)
  local copies, waits for them, and re-layouts  125 us (25%)
  starting transfers between devices  82.8 us (17%)
  other arithmetic  53.5 us (11%)
  matrix products  48.5 us (10%)
  between operations  17.1 us (3%)
    all_gather x1, waiting for transfers between devices, per_device(): whole = lax.all_gather(piece, AXES, axis=0, tiled=False)  80 us
    ppermute x27, starting transfers between devices, scatter_sum(): total = total + lax.ppermute(piece, axis, shift(axis, step)).astype(F32)  41.1 us
    all_to_all x7, waiting for transfers between devices, exchange(): return lax.all_to_all(value, axis, split_axis=0, concat_axis=0, tiled=True)  35.3 us
    ppermute x27, waiting for transfers between devices, scatter_sum(): total = total + lax.ppermute(piece, axis, shift(axis, step)).astype(F32)  28.4 us
    all_to_all x7, starting transfers between devices, exchange(): return lax.all_to_all(value, axis, split_axis=0, concat_axis=0, tiled=True)  26.4 us
    unnamed x202, local copies, waits for them, and re-layouts  18.1 us
    dot_general x15, matrix products, mm(): return jnp.dot(left, right, preferred_element_type=F32)  15.9 us
    reshape x3, local copies, waits for them, and re-layouts, column_chunks(): return part.reshape(4, 192, blocks_of, HALF).transpose(2, 0, 1, 3)  13.4 us
  transfers between devices with their start and end apart: 55, of which 32 were waited for; matrix products, arithmetic and copies ran while one was open for 25% of the time, Pallas kernels for 0%

profile of v1, /device:TPU:0, one launch (start us, length us, event | category | flops | bytes accessed | tf_op | source)
XLA Modules:
  0.0 491.1 jit_solution(6988477871523546274)
XLA Ops:
  11.1 4.4 all-to-all-start
  15.6 6.2 %all-to-all-done = bf16[8,3,6,384]{3,2,1,0:T(8,128)(2,1)S(1)} async-done(((bf16[8,3,6,384]{3,2,1,0:T(8,128)(2,1)}), bf16[8,3,6,384]{3,2,1,0:T(8,128)(2,1)S(1)}, u32[]{:S(2)}, u32[]{:S(2)}) %all-to-all-start) | async-done | bytes 110624 | tf_op jit(solution)/shard_map/all_to_all | solution.py:81
  29.1 80.0 %all-gather.3.cloned.1.call-done = bf16[26624,384]{1,0:T(8,128)(2,1)} async-done(((bf16[208,384]{1,0:T(8,128)(2,1)}), bf16[26624,384]{1,0:T(8,128)(2,1)}) %all-gather.3.cloned.1.call-update) | async-done | bytes 20447248 | tf_op jit(solution)/shard_map/all_gather | solution.py:178
  109.0 8.8 %dynamic-slice_bitcast_fusion.1 = bf16[16,4,208,384]{3,2,1,0:T(8,128)(2,1)} fusion(bf16[16,4,2,208,384]{4,3,2,1,0:T(8,128)(2,1)} %bitcast.401, s32[]{:T(128)S(6)} %select_n.389), kind=kLoop, calls=%fused_computation.4 | loop fusion | bytes 20447236 | tf_op jit(solution)/shard_map/jit(dynamic_index_in_dim)/squeeze | solution.py:198
  117.8 2.9 slice_bitcast_fusion.2
  120.7 4.2 slice_bitcast_fusion.1
  126.8 2.6 fusion.146
  145.5 8.8 %dynamic-slice_bitcast_fusion = bf16[4,16,208,384]{3,2,1,0:T(8,128)(2,1)} fusion(bf16[4,2,16,208,384]{4,3,2,1,0:T(8,128)(2,1)} %bitcast.403, s32[]{:T(128)S(6)} %select_n.389), kind=kLoop, calls=%fused_computation.3 | loop fusion | bytes 20447236 | tf_op jit(solution)/shard_map/jit(dynamic_index_in_dim)/squeeze | solution.py:203
  157.9 2.8 copy.368
  173.2 2.4 multiply_convert_fusion.1
  179.5 4.3 reshape.644
  195.6 4.1 reshape.645
  199.7 5.7 %constant_dynamic-slice_fusion.6 = (bf16[4,192,1,384]{3,2,1,0:T(2,128)(2,1)}, bf16[4,192,1,384]{3,2,1,0:T(2,128)(2,1)S(1)}, bf16[4,192,1,384]{3,2,1,0:T(2,128)(2,1)S(1)}, bf16[4,192,1,384]{3,2,1,0:T(2,128)(2,1)S(1)}) fusion(bf16[4,192,4,384]{3,2,1,0:T(4,128)(2,1)S(1)} %reshape.645, s32[]{:T(128)S(6)} %select_n.399, s32[]{:T(128)S(6)} %select_n.403, ...), kind=kLoop, calls=%fused_computation.282 | loop fusion | bytes 4718608 | tf_op jit(solution)/shard_map/dynamic-slice.4
  212.9 2.8 convolution_convert_fusion.4
  218.0 3.2 convolution_add_fusion.2
  226.6 2.5 reshape.648
  236.4 2.7 collective-permute-start.26
  254.3 3.8 convolution_convert_fusion.3
  258.1 4.9 %reshape.641 = bf16[4,192,3,384]{3,2,1,0:T(4,128)(2,1)} reshape(bf16[768,1152]{1,0:T(8,128)(2,1)} %convolution_convert_fusion.3) | data formatting | bytes 3538944 | tf_op jit(solution)/shard_map/reshape | solution.py:255
  266.2 2.5 convolution_convert_fusion.5
  268.7 2.5 reshape.642
  277.1 2.9 collective-permute-start.17
  281.5 4.2 fusion.3
  285.8 4.9 %constant_dynamic-slice_fusion.13 = (bf16[1,4,208,384]{3,0,2,1:T(2,128)(2,1)S(1)}, bf16[1,4,208,384]{3,0,2,1:T(2,128)(2,1)S(1)}, bf16[1,4,208,384]{3,0,2,1:T(2,128)(2,1)S(1)}, f32[1,4,208,384]{3,0,2,1:T(1,128)S(1)}) fusion(bf16[4,4,208,384]{3,0,2,1:T(4,128)(2,1)S(1)} %fusion.3, s32[]{:T(128)S(6)} %select_n.401, s32[]{:T(128)S(6)} %select_n.405, ...), kind=kLoop, calls=%fused_computation.289 | loop fusion | flops 319488 | bytes 5750800 | tf_op jit(solution)/shard_map/jit(dynamic_index_in_dim)/dynamic_slice | solution.py:59
  293.3 2.7 collective-permute-start.8
  300.1 2.6 collective-permute-start.23
  311.5 13.4 %collective-permute-done.7 = bf16[4,208,384]{2,1,0:T(8,128)(2,1)S(1)} collective-permute-done((bf16[4,208,384]{2,1,0:T(8,128)(2,1)S(1)}, bf16[4,208,384]{2,1,0:T(8,128)(2,1)S(1)}, u32[]{:S(2)}, u32[]{:S(2)}) %collective-permute-start.7) | collective-permute-done | bytes 639008 | tf_op jit(solution)/shard_map/ppermute | solution.py:60
  335.0 3.2 collective-permute-done.12
  345.6 3.7 collective-permute-done.31
  360.3 4.0 all-to-all-start.1
  366.7 3.7 all-to-all-done.1
  372.1 3.5 all-to-all-start.2
  375.6 6.0 %all-to-all-done.2 = bf16[4,4,6,768]{3,1,2,0:T(4,128)(2,1)S(1)} async-done(((bf16[4,4,6,768]{3,1,2,0:T(4,128)(2,1)}), bf16[4,4,6,768]{3,1,2,0:T(4,128)(2,1)S(1)}, u32[]{:S(2)}, u32[]{:S(2)}) %all-to-all-start.2) | async-done | bytes 147488 | tf_op jit(solution)/shard_map/all_to_all | solution.py:81
  385.0 3.5 all-to-all-start.3
  390.4 4.9 %all-to-all-done.3 = f32[4,4,6,768]{3,1,2,0:T(4,128)S(1)} async-done(((f32[4,4,6,768]{3,1,2,0:T(4,128)}), f32[4,4,6,768]{3,1,2,0:T(4,128)S(1)}, u32[]{:S(2)}, u32[]{:S(2)}) %all-to-all-start.3) | async-done | bytes 294944 | tf_op jit(solution)/shard_map/all_to_all | solution.py:81
  396.2 3.5 all-to-all-start.4
  401.3 5.1 %all-to-all-done.4 = f32[4,4,6,768]{3,1,2,0:T(4,128)S(1)} async-done(((f32[4,4,6,768]{3,1,2,0:T(4,128)}), f32[4,4,6,768]{3,1,2,0:T(4,128)S(1)}, u32[]{:S(2)}, u32[]{:S(2)}) %all-to-all-start.4) | async-done | bytes 294944 | tf_op jit(solution)/shard_map/all_to_all | solution.py:81
  407.2 2.9 collective-permute-start.37
  422.2 2.7 collective-permute-start.41
  425.8 3.0 collective-permute-done.40
  428.7 2.5 collective-permute-done.41
  433.1 2.9 collective-permute-start.44
  437.1 3.0 collective-permute-done.43
  444.9 6.8 %gather_fusion = bf16[768]{0:T(1024)(128)(2,1)S(1)} fusion(bf16[768,768]{1,0:T(8,128)(2,1)S(1)} %bitcast.397, s32[768]{0:T(1024)S(1)} %or_reduce_fusion), kind=kCustom, calls=%fused_computation | custom fusion | bytes 9216 | tf_op jit(solution)/shard_map/jit(diagonal)/cond/branch_0_fun/gather | solution.py:361
  460.3 4.2 all-to-all-start.5
  465.2 5.3 %all-to-all-done.5 = bf16[4,4,6,768]{3,1,2,0:T(4,128)(2,1)S(1)} async-done(((bf16[4,4,6,768]{3,1,2,0:T(4,128)(2,1)}), bf16[4,4,6,768]{3,1,2,0:T(4,128)(2,1)S(1)}, u32[]{:S(2)}, u32[]{:S(2)}) %all-to-all-start.5) | async-done | bytes 147488 | tf_op jit(solution)/shard_map/all_to_all | solution.py:81
  471.3 3.5 all-to-all-start.6
  476.7 4.1 all-to-all-done.6
  (506 shorter events, 199.6 us)
Async XLA Ops:
  11.1 10.7 %all-to-all-start = ((bf16[8,3,6,384]{3,2,1,0:T(8,128)(2,1)}), bf16[8,3,6,384]{3,2,1,0:T(8,128)(2,1)S(1)}, u32[]{:S(2)}, u32[]{:S(2)}) async-start(bf16[8,3,6,384]{3,2,1,0:T(8,128)(2,1)} %copy.355), calls=%async_computation | async-start | bytes 294912 | tf_op jit(solution)/shard_map/all_to_all | solution.py:81
  15.4 93.6 %all-gather.3.cloned.1.call-start = ((), (), s32[]{:S(2)}) async-start(), calls=%async_computation.7 | async-start | bytes 20606976 | tf_op jit(solution)/shard_map/all_gather | solution.py:178
  145.1 21.5 %collective-permute-start.2 = (bf16[256,384]{0,1:T(8,128)(2,1)}, bf16[256,384]{0,1:T(8,128)(2,1)}, u32[]{:S(2)}, u32[]{:S(2)}) collective-permute-start(bf16[256,384]{0,1:T(8,128)(2,1)} %bitcast.395), channel_id=1, source_target_pairs={{0,1},{1,0},{2,3},{3,2},{4,5},{5,4},{6,7},{7,6},{8,9},{9,8},{10,11... | collective-permute-start | bytes 589832 | tf_op jit(solution)/shard_map/ppermute | solution.py:44
  186.5 36.9 %collective-permute-start.13 = (bf16[4,192,384]{2,1,0:T(8,128)(2,1)}, bf16[4,192,384]{2,1,0:T(8,128)(2,1)}, u32[]{:S(2)}, u32[]{:S(2)}) collective-permute-start(bf16[4,192,384]{2,1,0:T(8,128)(2,1)} %bitcast.391), channel_id=1, source_target_pairs={{0,2},{2,4},{4,6},{6,0},{1,3},{3,5},{5,7},{7,1},{8,10},{10,12},{12... | collective-permute-start | bytes 1769480 | tf_op jit(solution)/shard_map/ppermute | solution.py:60
  188.8 44.3 %collective-permute-start.14 = (bf16[4,192,384]{2,1,0:T(8,128)(2,1)}, bf16[4,192,384]{2,1,0:T(8,128)(2,1)}, u32[]{:S(2)}, u32[]{:S(2)}) collective-permute-start(bf16[4,192,384]{2,1,0:T(8,128)(2,1)} %bitcast.390), channel_id=1, source_target_pairs={{0,6},{2,0},{4,2},{6,4},{1,7},{3,1},{5,3},{7,5},{8,14},{10,8},{12,... | collective-permute-start | bytes 1769480 | tf_op jit(solution)/shard_map/ppermute | solution.py:60
  191.5 42.2 %collective-permute-start.15 = (bf16[4,192,384]{2,1,0:T(8,128)(2,1)}, bf16[4,192,384]{2,1,0:T(8,128)(2,1)}, u32[]{:S(2)}, u32[]{:S(2)}) collective-permute-start(bf16[4,192,384]{2,1,0:T(8,128)(2,1)} %bitcast.389), channel_id=1, source_target_pairs={{0,4},{2,6},{4,0},{6,2},{1,5},{3,7},{5,1},{7,3},{8,12},{10,14},{12... | collective-permute-start | bytes 1769480 | tf_op jit(solution)/shard_map/ppermute | solution.py:60
  206.3 30.0 %collective-permute-start.19 = (bf16[4,192,384]{2,1,0:T(8,128)(2,1)}, bf16[4,192,384]{2,1,0:T(8,128)(2,1)}, u32[]{:S(2)}, u32[]{:S(2)}) collective-permute-start(bf16[4,192,384]{2,1,0:T(8,128)(2,1)} %bitcast.388), channel_id=1, source_target_pairs={{0,8},{8,16},{16,24},{24,0},{1,9},{9,17},{17,25},{25,1},{2,10},{10... | collective-permute-start | bytes 1769480 | tf_op jit(solution)/shard_map/ppermute | solution.py:60
  208.7 30.3 %collective-permute-start.20 = (bf16[4,192,384]{2,1,0:T(8,128)(2,1)}, bf16[4,192,384]{2,1,0:T(8,128)(2,1)}, u32[]{:S(2)}, u32[]{:S(2)}) collective-permute-start(bf16[4,192,384]{2,1,0:T(8,128)(2,1)} %bitcast.387), channel_id=1, source_target_pairs={{0,24},{8,0},{16,8},{24,16},{1,25},{9,1},{17,9},{25,17},{2,26},{10... | collective-permute-start | bytes 1769480 | tf_op jit(solution)/shard_map/ppermute | solution.py:60
  223.3 16.2 %collective-permute-start.21 = (bf16[4,192,384]{2,1,0:T(8,128)(2,1)}, bf16[4,192,384]{2,1,0:T(8,128)(2,1)}, u32[]{:S(2)}, u32[]{:S(2)}) collective-permute-start(bf16[4,192,384]{2,1,0:T(8,128)(2,1)} %bitcast.386), channel_id=1, source_target_pairs={{0,16},{8,24},{16,0},{24,8},{1,17},{9,25},{17,1},{25,9},{2,18},{10... | collective-permute-start | bytes 1769480 | tf_op jit(solution)/shard_map/ppermute | solution.py:60
  233.1 57.9 %collective-permute-start.25 = (bf16[4,192,384]{2,1,0:T(8,128)(2,1)}, bf16[4,192,384]{2,1,0:T(8,128)(2,1)}, u32[]{:S(2)}, u32[]{:S(2)}) collective-permute-start(bf16[4,192,384]{2,1,0:T(8,128)(2,1)} %get-tuple-element.96), channel_id=1, source_target_pairs={{0,2},{2,4},{4,6},{6,0},{1,3},{3,5},{5,7},{7,1},{8,10},{10,12},{12... | collective-permute-start | bytes 1769480 | tf_op jit(solution)/shard_map/ppermute | solution.py:60
  233.7 8.5 %collective-permute-start.5 = (f32[256,768]{1,0:T(8,128)S(1)}, f32[256,768]{1,0:T(8,128)S(1)}, u32[]{:S(2)}, u32[]{:S(2)}) collective-permute-start(f32[256,768]{1,0:T(8,128)S(1)} %copy-done.19), channel_id=1, source_target_pairs={{0,1},{1,0},{2,3},{3,2},{4,5},{5,4},{6,7},{7,6},{8,9},{9,8},{10,11... | collective-permute-start | bytes 2359304 | tf_op jit(solution)/shard_map/ppermute | solution.py:44
  236.4 56.0 %collective-permute-start.26 = (bf16[4,192,384]{2,1,0:T(8,128)(2,1)}, bf16[4,192,384]{2,1,0:T(8,128)(2,1)}, u32[]{:S(2)}, u32[]{:S(2)}) collective-permute-start(bf16[4,192,384]{2,1,0:T(8,128)(2,1)} %get-tuple-element.98), channel_id=1, source_target_pairs={{0,6},{2,0},{4,2},{6,4},{1,7},{3,1},{5,3},{7,5},{8,14},{10,8},{12,... | collective-permute-start | bytes 1769480 | tf_op jit(solution)/shard_map/ppermute | solution.py:60
  239.0 53.7 %collective-permute-start.27 = (bf16[4,192,384]{2,1,0:T(8,128)(2,1)}, bf16[4,192,384]{2,1,0:T(8,128)(2,1)}, u32[]{:S(2)}, u32[]{:S(2)}) collective-permute-start(bf16[4,192,384]{2,1,0:T(8,128)(2,1)} %get-tuple-element.97), channel_id=1, source_target_pairs={{0,4},{2,6},{4,0},{6,2},{1,5},{3,7},{5,1},{7,3},{8,12},{10,14},{12... | collective-permute-start | bytes 1769480 | tf_op jit(solution)/shard_map/ppermute | solution.py:60
  239.6 34.9 %collective-permute-start.3 = (f32[128,768]{1,0:T(8,128)}, f32[128,768]{1,0:T(8,128)}, u32[]{:S(2)}, u32[]{:S(2)}) collective-permute-start(f32[128,768]{1,0:T(8,128)} %constant_dynamic-slice_fusion.16), channel_id=1, source_target_pairs={{0,1},{1,0},{2,3},{3,2},{4,5},{5,4},{6,7},{7,6},{8,9},{9,8},{10,11... | collective-permute-start | bytes 1179656 | tf_op jit(solution)/shard_map/ppermute | solution.py:44
  265.7 11.3 %collective-permute-start.6 = (f32[128,768]{1,0:T(8,128)}, f32[128,768]{1,0:T(8,128)}, u32[]{:S(2)}, u32[]{:S(2)}) collective-permute-start(f32[128,768]{1,0:T(8,128)} %constant_dynamic-slice_fusion.14), channel_id=1, source_target_pairs={{0,1},{1,0},{2,3},{3,2},{4,5},{5,4},{6,7},{7,6},{8,9},{9,8},{10,11... | collective-permute-start | bytes 1179656 | tf_op jit(solution)/shard_map/ppermute | solution.py:44
  274.5 18.9 %collective-permute-start.16 = (bf16[192,384]{1,0:T(8,128)(2,1)}, bf16[192,384]{1,0:T(8,128)(2,1)S(1)}, u32[]{:S(2)}, u32[]{:S(2)}) collective-permute-start(bf16[192,384]{1,0:T(8,128)(2,1)} %get-tuple-element.110), channel_id=1, source_target_pairs={{0,8},{8,16},{16,24},{24,0},{1,9},{9,17},{17,25},{25,1},{2,10},{10... | collective-permute-start | bytes 442376 | tf_op jit(solution)/shard_map/ppermute | solution.py:60
  277.1 18.9 %collective-permute-start.17 = (bf16[192,384]{1,0:T(8,128)(2,1)S(1)}, bf16[192,384]{1,0:T(8,128)(2,1)S(1)}, u32[]{:S(2)}, u32[]{:S(2)}) collective-permute-start(bf16[192,384]{1,0:T(8,128)(2,1)S(1)} %copy-done.66), channel_id=1, source_target_pairs={{0,24},{8,0},{16,8},{24,16},{1,25},{9,1},{17,9},{25,17},{2,26},{10... | collective-permute-start | bytes 442376 | tf_op jit(solution)/shard_map/ppermute | solution.py:60
  291.8 8.3 %collective-permute-start.18 = (bf16[192,384]{1,0:T(8,128)(2,1)S(1)}, bf16[192,384]{1,0:T(8,128)(2,1)S(1)}, u32[]{:S(2)}, u32[]{:S(2)}) collective-permute-start(bf16[192,384]{1,0:T(8,128)(2,1)S(1)} %copy-done.63), channel_id=1, source_target_pairs={{0,16},{8,24},{16,0},{24,8},{1,17},{9,25},{17,1},{25,9},{2,18},{10... | collective-permute-start | bytes 442376 | tf_op jit(solution)/shard_map/ppermute | solution.py:60
  292.4 10.3 %collective-permute-start.22 = (bf16[192,384]{1,0:T(8,128)(2,1)S(1)}, bf16[192,384]{1,0:T(8,128)(2,1)S(1)}, u32[]{:S(2)}, u32[]{:S(2)}) collective-permute-start(bf16[192,384]{1,0:T(8,128)(2,1)S(1)} %copy-done.67), channel_id=1, source_target_pairs={{0,2},{2,4},{4,6},{6,0},{1,3},{3,5},{5,7},{7,1},{8,10},{10,12},{12... | collective-permute-start | bytes 442376 | tf_op jit(solution)/shard_map/ppermute | solution.py:60
  292.8 32.1 %collective-permute-start.7 = (bf16[4,208,384]{2,1,0:T(8,128)(2,1)S(1)}, bf16[4,208,384]{2,1,0:T(8,128)(2,1)S(1)}, u32[]{:S(2)}, u32[]{:S(2)}) collective-permute-start(bf16[4,208,384]{2,1,0:T(8,128)(2,1)S(1)} %bitcast.469), channel_id=1, source_target_pairs={{0,8},{8,16},{16,24},{24,0},{1,9},{9,17},{17,25},{25,1},{2,10},{10... | collective-permute-start | bytes 1916936 | tf_op jit(solution)/shard_map/ppermute | solution.py:60
  293.3 33.5 %collective-permute-start.8 = (bf16[4,208,384]{2,1,0:T(8,128)(2,1)S(1)}, bf16[4,208,384]{2,1,0:T(8,128)(2,1)S(1)}, u32[]{:S(2)}, u32[]{:S(2)}) collective-permute-start(bf16[4,208,384]{2,1,0:T(8,128)(2,1)S(1)} %bitcast.468), channel_id=1, source_target_pairs={{0,24},{8,0},{16,8},{24,16},{1,25},{9,1},{17,9},{25,17},{2,26},{10... | collective-permute-start | bytes 1916936 | tf_op jit(solution)/shard_map/ppermute | solution.py:60
  296.0 31.6 %collective-permute-start.9 = (bf16[4,208,384]{2,1,0:T(8,128)(2,1)S(1)}, bf16[4,208,384]{2,1,0:T(8,128)(2,1)S(1)}, u32[]{:S(2)}, u32[]{:S(2)}) collective-permute-start(bf16[4,208,384]{2,1,0:T(8,128)(2,1)S(1)} %bitcast.467), channel_id=1, source_target_pairs={{0,16},{8,24},{16,0},{24,8},{1,17},{9,25},{17,1},{25,9},{2,18},{10... | collective-permute-start | bytes 1916936 | tf_op jit(solution)/shard_map/ppermute | solution.py:60
  300.1 7.1 %collective-permute-start.23 = (bf16[192,384]{1,0:T(8,128)(2,1)S(1)}, bf16[192,384]{1,0:T(8,128)(2,1)S(1)}, u32[]{:S(2)}, u32[]{:S(2)}) collective-permute-start(bf16[192,384]{1,0:T(8,128)(2,1)S(1)} %copy-done.65), channel_id=1, source_target_pairs={{0,6},{2,0},{4,2},{6,4},{1,7},{3,1},{5,3},{7,5},{8,14},{10,8},{12,... | collective-permute-start | bytes 442376 | tf_op jit(solution)/shard_map/ppermute | solution.py:60
  302.7 6.6 %collective-permute-start.24 = (bf16[192,384]{1,0:T(8,128)(2,1)S(1)}, bf16[192,384]{1,0:T(8,128)(2,1)S(1)}, u32[]{:S(2)}, u32[]{:S(2)}) collective-permute-start(bf16[192,384]{1,0:T(8,128)(2,1)S(1)} %copy-done.64), channel_id=1, source_target_pairs={{0,4},{2,6},{4,0},{6,2},{1,5},{3,7},{5,1},{7,3},{8,12},{10,14},{12... | collective-permute-start | bytes 442376 | tf_op jit(solution)/shard_map/ppermute | solution.py:60
  307.2 24.2 %collective-permute-start.28 = (bf16[192,384]{1,0:T(8,128)(2,1)S(1)}, bf16[192,384]{1,0:T(8,128)(2,1)S(1)}, u32[]{:S(2)}, u32[]{:S(2)}) collective-permute-start(bf16[192,384]{1,0:T(8,128)(2,1)S(1)} %get-tuple-element.116), channel_id=1, source_target_pairs={{0,8},{8,16},{16,24},{24,0},{1,9},{9,17},{17,25},{25,1},{2,10},{10... | collective-permute-start | bytes 442376 | tf_op jit(solution)/shard_map/ppermute | solution.py:60
  309.4 24.2 %collective-permute-start.29 = (bf16[192,384]{1,0:T(8,128)(2,1)S(1)}, bf16[192,384]{1,0:T(8,128)(2,1)S(1)}, u32[]{:S(2)}, u32[]{:S(2)}) collective-permute-start(bf16[192,384]{1,0:T(8,128)(2,1)S(1)} %get-tuple-element.118), channel_id=1, source_target_pairs={{0,24},{8,0},{16,8},{24,16},{1,25},{9,1},{17,9},{25,17},{2,26},{10... | collective-permute-start | bytes 442376 | tf_op jit(solution)/shard_map/ppermute | solution.py:60
  324.9 8.8 %collective-permute-start.30 = (bf16[192,384]{1,0:T(8,128)(2,1)S(1)}, bf16[192,384]{1,0:T(8,128)(2,1)S(1)}, u32[]{:S(2)}, u32[]{:S(2)}) collective-permute-start(bf16[192,384]{1,0:T(8,128)(2,1)S(1)} %get-tuple-element.117), channel_id=1, source_target_pairs={{0,16},{8,24},{16,0},{24,8},{1,17},{9,25},{17,1},{25,9},{2,18},{10... | collective-permute-start | bytes 442376 | tf_op jit(solution)/shard_map/ppermute | solution.py:60
  327.9 6.7 %collective-permute-start.10 = (bf16[208,384]{1,0:T(8,128)(2,1)S(1)}, bf16[208,384]{1,0:T(8,128)(2,1)S(1)}, u32[]{:S(2)}, u32[]{:S(2)}) collective-permute-start(bf16[208,384]{1,0:T(8,128)(2,1)S(1)} %get-tuple-element.107), channel_id=1, source_target_pairs={{0,2},{2,4},{4,6},{6,0},{1,3},{3,5},{5,7},{7,1},{8,10},{10,12},{12... | collective-permute-start | bytes 479240 | tf_op jit(solution)/shard_map/ppermute | solution.py:60
  331.4 6.8 %collective-permute-start.12 = (bf16[208,384]{1,0:T(8,128)(2,1)S(1)}, bf16[208,384]{1,0:T(8,128)(2,1)S(1)}, u32[]{:S(2)}, u32[]{:S(2)}) collective-permute-start(bf16[208,384]{1,0:T(8,128)(2,1)S(1)} %get-tuple-element.108), channel_id=1, source_target_pairs={{0,4},{2,6},{4,0},{6,2},{1,5},{3,7},{5,1},{7,3},{8,12},{10,14},{12... | collective-permute-start | bytes 479240 | tf_op jit(solution)/shard_map/ppermute | solution.py:60
  340.9 8.3 %collective-permute-start.31 = (bf16[208,384]{1,0:T(8,128)(2,1)}, bf16[208,384]{1,0:T(8,128)(2,1)S(1)}, u32[]{:S(2)}, u32[]{:S(2)}) collective-permute-start(bf16[208,384]{1,0:T(8,128)(2,1)} %get-tuple-element.104), channel_id=1, source_target_pairs={{0,32},{32,64},{64,96},{96,0},{1,33},{33,65},{65,97},{97,1},{2,34}... | collective-permute-start | bytes 479240 | tf_op jit(solution)/shard_map/ppermute | solution.py:60
  342.0 7.4 %collective-permute-start.32 = (bf16[208,384]{1,0:T(8,128)(2,1)}, bf16[208,384]{1,0:T(8,128)(2,1)}, u32[]{:S(2)}, u32[]{:S(2)}) collective-permute-start(bf16[208,384]{1,0:T(8,128)(2,1)} %get-tuple-element.106), channel_id=1, source_target_pairs={{0,96},{32,0},{64,32},{96,64},{1,97},{33,1},{65,33},{97,65},{2,98}... | collective-permute-start | bytes 479240 | tf_op jit(solution)/shard_map/ppermute | solution.py:60
  344.2 6.9 %collective-permute-start.33 = (bf16[208,384]{1,0:T(8,128)(2,1)S(1)}, bf16[208,384]{1,0:T(8,128)(2,1)}, u32[]{:S(2)}, u32[]{:S(2)}) collective-permute-start(bf16[208,384]{1,0:T(8,128)(2,1)S(1)} %get-tuple-element.105), channel_id=1, source_target_pairs={{0,64},{32,96},{64,0},{96,32},{1,65},{33,97},{65,1},{97,33},{2,66}... | collective-permute-start | bytes 479240 | tf_op jit(solution)/shard_map/ppermute | solution.py:60
  360.3 10.1 %all-to-all-start.1 = ((bf16[4,4,6,768]{3,1,2,0:T(4,128)(2,1)}), bf16[4,4,6,768]{3,1,2,0:T(4,128)(2,1)}, u32[]{:S(2)}, u32[]{:S(2)}) async-start(bf16[4,4,6,768]{3,1,2,0:T(4,128)(2,1)} %fusion.84), calls=%async_computation.1 | async-start | bytes 294912 | tf_op jit(solution)/shard_map/all_to_all | solution.py:81
  372.1 9.5 %all-to-all-start.2 = ((bf16[4,4,6,768]{3,1,2,0:T(4,128)(2,1)}), bf16[4,4,6,768]{3,1,2,0:T(4,128)(2,1)S(1)}, u32[]{:S(2)}, u32[]{:S(2)}) async-start(bf16[4,4,6,768]{3,1,2,0:T(4,128)(2,1)} %bitcast_select_fusion.2), calls=%async_computation.2 | async-start | bytes 294912 | tf_op jit(solution)/shard_map/all_to_all | solution.py:81
  385.0 10.3 %all-to-all-start.3 = ((f32[4,4,6,768]{3,1,2,0:T(4,128)}), f32[4,4,6,768]{3,1,2,0:T(4,128)S(1)}, u32[]{:S(2)}, u32[]{:S(2)}) async-start(f32[4,4,6,768]{3,1,2,0:T(4,128)} %copy.410), calls=%async_computation.3 | async-start | bytes 589824 | tf_op jit(solution)/shard_map/all_to_all | solution.py:81
  396.2 10.3 %all-to-all-start.4 = ((f32[4,4,6,768]{3,1,2,0:T(4,128)}), f32[4,4,6,768]{3,1,2,0:T(4,128)S(1)}, u32[]{:S(2)}, u32[]{:S(2)}) async-start(f32[4,4,6,768]{3,1,2,0:T(4,128)} %bitcast_select_fusion), calls=%async_computation.4 | async-start | bytes 589824 | tf_op jit(solution)/shard_map/all_to_all | solution.py:81
  400.4 16.5 %collective-permute-start.34 = (f32[2,6]{1,0:T(2,128)S(1)}, f32[2,6]{1,0:T(2,128)S(1)}, u32[]{:S(2)}, u32[]{:S(2)}) collective-permute-start(f32[2,6]{1,0:T(2,128)S(1)} %bitcast.485), channel_id=1, source_target_pairs={{0,1},{1,0},{2,3},{3,2},{4,5},{5,4},{6,7},{7,6},{8,9},{9,8},{10,11... | collective-permute-start | bytes 152 | tf_op jit(solution)/shard_map/ppermute | solution.py:44
  406.9 6.4 %collective-permute-start.36 = (bf16[96,768]{1,0:T(8,128)(2,1)S(1)}, bf16[96,768]{1,0:T(8,128)(2,1)S(1)}, u32[]{:S(2)}, u32[]{:S(2)}) collective-permute-start(bf16[96,768]{1,0:T(8,128)(2,1)S(1)} %fusion.87), channel_id=1, source_target_pairs={{0,2},{2,4},{4,6},{6,0},{1,3},{3,5},{5,7},{7,1},{8,10},{10,12},{12... | collective-permute-start | bytes 442376 | tf_op jit(solution)/shard_map/ppermute | solution.py:69
  407.2 7.2 %collective-permute-start.37 = (bf16[96,768]{1,0:T(8,128)(2,1)S(1)}, bf16[96,768]{1,0:T(8,128)(2,1)S(1)}, u32[]{:S(2)}, u32[]{:S(2)}) collective-permute-start(bf16[96,768]{1,0:T(8,128)(2,1)S(1)} %fusion.87), channel_id=1, source_target_pairs={{0,6},{2,0},{4,2},{6,4},{1,7},{3,1},{5,3},{7,5},{8,14},{10,8},{12,... | collective-permute-start | bytes 442376 | tf_op jit(solution)/shard_map/ppermute | solution.py:69
  410.2 6.6 %collective-permute-start.38 = (bf16[96,768]{1,0:T(8,128)(2,1)S(1)}, bf16[96,768]{1,0:T(8,128)(2,1)S(1)}, u32[]{:S(2)}, u32[]{:S(2)}) collective-permute-start(bf16[96,768]{1,0:T(8,128)(2,1)S(1)} %fusion.87), channel_id=1, source_target_pairs={{0,4},{2,6},{4,0},{6,2},{1,5},{3,7},{5,1},{7,3},{8,12},{10,14},{12... | collective-permute-start | bytes 442376 | tf_op jit(solution)/shard_map/ppermute | solution.py:69
  421.5 7.2 %collective-permute-start.40 = (bf16[96,768]{1,0:T(8,128)(2,1)S(1)}, bf16[96,768]{1,0:T(8,128)(2,1)S(1)}, u32[]{:S(2)}, u32[]{:S(2)}) collective-permute-start(bf16[96,768]{1,0:T(8,128)(2,1)S(1)} %fusion.80), channel_id=1, source_target_pairs={{0,8},{8,16},{16,24},{24,0},{1,9},{9,17},{17,25},{25,1},{2,10},{10... | collective-permute-start | bytes 442376 | tf_op jit(solution)/shard_map/ppermute | solution.py:358
  422.2 9.0 %collective-permute-start.41 = (bf16[96,768]{1,0:T(8,128)(2,1)S(1)}, bf16[96,768]{1,0:T(8,128)(2,1)S(1)}, u32[]{:S(2)}, u32[]{:S(2)}) collective-permute-start(bf16[96,768]{1,0:T(8,128)(2,1)S(1)} %fusion.80), channel_id=1, source_target_pairs={{0,24},{8,0},{16,8},{24,16},{1,25},{9,1},{17,9},{25,17},{2,26},{10... | collective-permute-start | bytes 442376 | tf_op jit(solution)/shard_map/ppermute | solution.py:358
  424.8 7.1 %collective-permute-start.42 = (bf16[96,768]{1,0:T(8,128)(2,1)S(1)}, bf16[96,768]{1,0:T(8,128)(2,1)S(1)}, u32[]{:S(2)}, u32[]{:S(2)}) collective-permute-start(bf16[96,768]{1,0:T(8,128)(2,1)S(1)} %fusion.80), channel_id=1, source_target_pairs={{0,16},{8,24},{16,0},{24,8},{1,17},{9,25},{17,1},{25,9},{2,18},{10... | collective-permute-start | bytes 442376 | tf_op jit(solution)/shard_map/ppermute | solution.py:358
  432.1 8.0 %collective-permute-start.43 = (bf16[96,768]{1,0:T(8,128)(2,1)S(1)}, bf16[96,768]{1,0:T(8,128)(2,1)S(1)}, u32[]{:S(2)}, u32[]{:S(2)}) collective-permute-start(bf16[96,768]{1,0:T(8,128)(2,1)S(1)} %get-tuple-element.73), channel_id=1, source_target_pairs={{0,2},{2,4},{4,6},{6,0},{1,3},{3,5},{5,7},{7,1},{8,10},{10,12},{12... | collective-permute-start | bytes 442376 | tf_op jit(solution)/shard_map/ppermute | solution.py:69
  433.1 7.8 %collective-permute-start.44 = (bf16[96,768]{1,0:T(8,128)(2,1)S(1)}, bf16[96,768]{1,0:T(8,128)(2,1)S(1)}, u32[]{:S(2)}, u32[]{:S(2)}) collective-permute-start(bf16[96,768]{1,0:T(8,128)(2,1)S(1)} %get-tuple-element.73), channel_id=1, source_target_pairs={{0,6},{2,0},{4,2},{6,4},{1,7},{3,1},{5,3},{7,5},{8,14},{10,8},{12,... | collective-permute-start | bytes 442376 | tf_op jit(solution)/shard_map/ppermute | solution.py:69
  436.0 6.6 %collective-permute-start.45 = (bf16[96,768]{1,0:T(8,128)(2,1)S(1)}, bf16[96,768]{1,0:T(8,128)(2,1)S(1)}, u32[]{:S(2)}, u32[]{:S(2)}) collective-permute-start(bf16[96,768]{1,0:T(8,128)(2,1)S(1)} %get-tuple-element.73), channel_id=1, source_target_pairs={{0,4},{2,6},{4,0},{6,2},{1,5},{3,7},{5,1},{7,3},{8,12},{10,14},{12... | collective-permute-start | bytes 442376 | tf_op jit(solution)/shard_map/ppermute | solution.py:69
  460.3 10.3 %all-to-all-start.5 = ((bf16[4,4,6,768]{3,1,2,0:T(4,128)(2,1)}), bf16[4,4,6,768]{3,1,2,0:T(4,128)(2,1)S(1)}, u32[]{:S(2)}, u32[]{:S(2)}) async-start(bf16[4,4,6,768]{3,1,2,0:T(4,128)(2,1)} %copy.422), calls=%async_computation.5 | async-start | bytes 294912 | tf_op jit(solution)/shard_map/all_to_all | solution.py:81
  471.3 9.5 %all-to-all-start.6 = ((bf16[4,4,6,768]{3,1,2,0:T(4,128)(2,1)}), bf16[4,4,6,768]{3,1,2,0:T(4,128)(2,1)S(1)}, u32[]{:S(2)}, u32[]{:S(2)}) async-start(bf16[4,4,6,768]{3,1,2,0:T(4,128)(2,1)} %bitcast_select_fusion.1), calls=%async_computation.6 | async-start | bytes 294912 | tf_op jit(solution)/shard_map/all_to_all | solution.py:81
  (98 other events, 539.8 us)
Sparse Core Ops, SparseCore 0:
  22.7 86.3 all-gather.2
